TPU v7x, 512 devices: a whole 4x8x8 slice. The times are simulated.
512 devices in a mesh: row: 64 (over y, z_lo, core), col: 8 (over z_hi, x).
Axes of the slice: x: 4, y: 8, z: 8 (z_hi: 2, z_lo: 4; z = z_hi * 4 + z_lo), core: 2. Of those that a mesh axis runs over, the one named last changes fastest.
Arguments:
- telemetry: float32 [8, 2048, 64], P('col', 'row'), may hold values from -6 to 6
- target: int32 [8, 2048], P('col', 'row'), may hold values from 0 to 8191, as said below
- counts: int32 [8, 64], P('col', 'row'), may hold values from 0 to 32, as said below
- lengthscale: float32 [64], replicated, may hold values from 2 to 8
- nugget: float32 [8192], P('row'), may hold values from 0.1 to 1
Outputs:
- schur: float32 [8192, 8, 1024], P('row', 'col')
- lower_col: float32 [8192, 1024], P('row')
Inputs may be any that keep to these rules, and one draw needn't show every extreme that they name: `target`: the first counts slots of each device hold distinct location indices, and over all devices every location appears exactly once among them; later slots hold arbitrary indices. The used slots of device (c, r) name only locations of row blocks (r - d) mod 64 with 0 <= d < 16, at most 2 locations of any one row block, and exactly 2 for every block they name. `counts`: Even; 32 on some device of every index of col; the total over all devices is 8192.
All inputs are finite; a program needn't handle non-finite values.
Results may differ from a plain program's by a relative error of at most 0.0003.
Values sent between devices are 32-bit elements; how exact they have to be, the bound alone decides.
A program may use at most 128 MiB of HBM per device.

v0:
```python
import jax
import jax.numpy as jnp
from jax import lax
from jax.sharding import PartitionSpec as P

F = 64
PB = 1024
RB = 128


root_three = 1.7320508075688772


def passed_along(block, axis, distance):
    devices = range(lax.axis_size(axis))
    route = [((i - distance) % len(devices), i) for i in devices]
    return lax.ppermute(block, axis, route)


def matern(left, right, inv_len):
    left_s = left * inv_len
    right_s = right * inv_len
    inner = jnp.dot(
        left_s, right_s.T, precision=lax.Precision.HIGHEST, preferred_element_type=jnp.float32
    )
    squared = (
        jnp.sum(left_s * left_s, axis=1)[:, None]
        + jnp.sum(right_s * right_s, axis=1)[None, :]
        - 2.0 * inner
    )
    distance = jnp.sqrt(jnp.maximum(squared, 0.0))
    return (1.0 + root_three * distance) * jnp.exp(-root_three * distance)


def body(telemetry, target, counts, lengthscale, nugget):
    row_count = lax.axis_size("row")
    col_count = lax.axis_size("col")
    row_index = lax.axis_index("row")
    col_index = lax.axis_index("col")
    slice_len = RB // col_count
    send_cap = 2 * max(1, slice_len // row_count)
    window = min(row_count, slice_len)
    readings = telemetry[0]
    listing = target[0]
    filled = counts[0, 0]
    in_slots = readings.shape[0]
    slot_ids = jnp.arange(in_slots, dtype=jnp.int32)
    in_use = slot_ids < filled
    zone_owner = listing // RB
    offset = (row_index - zone_owner) % row_count
    earlier = (
        (zone_owner[:, None] == zone_owner[None, :])
        & in_use[None, :]
        & (slot_ids[None, :] < slot_ids[:, None])
    )
    position = jnp.sum(earlier.astype(jnp.int32), axis=1)
    keep = in_use & (position < send_cap) & (offset < window)
    send_slot = jnp.where(keep, offset * send_cap + position, -1)
    outgoing = jnp.arange(window * send_cap, dtype=jnp.int32)
    picker = outgoing[:, None] == send_slot[None, :]
    rows_buf = jnp.dot(
        picker.astype(jnp.float32),
        readings,
        precision=lax.Precision.HIGHEST,
        preferred_element_type=jnp.float32,
    ).reshape(window, send_cap, F)
    local_place = (listing % RB).astype(jnp.float32)
    place_buf = jnp.max(jnp.where(picker, local_place[None, :], -1.0), axis=1).reshape(
        window, send_cap
    )
    for level in range(window.bit_length() - 1):
        stride = 1 << level
        rows_split = rows_buf.reshape(window // (2 * stride), 2, stride, send_cap, F)
        place_split = place_buf.reshape(window // (2 * stride), 2, stride, send_cap)
        moved_rows, moved_place = passed_along(
            (rows_split[:, 1], place_split[:, 1]), "row", -stride
        )
        rows_buf = jnp.stack([rows_split[:, 0], moved_rows], axis=1).reshape(window, send_cap, F)
        place_buf = jnp.stack([place_split[:, 0], moved_place], axis=1).reshape(window, send_cap)
    got_ids = place_buf.reshape(-1).astype(jnp.int32)
    block_ids = jnp.arange(RB, dtype=jnp.int32)
    placer = (block_ids[:, None] == got_ids[None, :]).astype(jnp.float32)
    partial_block = jnp.dot(
        placer,
        rows_buf.reshape(window * send_cap, F),
        precision=lax.Precision.HIGHEST,
        preferred_element_type=jnp.float32,
    )
    block_pts = lax.psum(partial_block, "col")
    inv_len = 1.0 / lengthscale
    my_pts = lax.dynamic_slice_in_dim(block_pts, col_index * slice_len, slice_len, 0)
    my_nug = lax.dynamic_slice_in_dim(nugget, col_index * slice_len, slice_len, 0)
    start_row = jnp.minimum(row_index * RB, PB - RB)
    in_panel = (row_index * RB < PB).astype(jnp.float32)
    panel_buf = lax.dynamic_update_slice(
        jnp.zeros((PB, F), jnp.float32), block_pts * in_panel, (start_row, 0)
    )
    nugget_buf = lax.dynamic_update_slice(
        jnp.zeros((PB,), jnp.float32), nugget * in_panel, (start_row,)
    )
    panel_pts, panel_nug = lax.psum((panel_buf, nugget_buf), "row")
    column_pts, column_nug = (
        lax.all_gather(my_pts, "row", axis=0, tiled=True),
        lax.all_gather(my_nug, "row", axis=0, tiled=True),
    )
    panel_ids = jnp.arange(PB, dtype=jnp.int32)
    panel_kernel = matern(panel_pts, panel_pts, inv_len) + jnp.diag(panel_nug)
    factor = jnp.linalg.cholesky(panel_kernel)
    my_ids = row_index * RB + col_index * slice_len + jnp.arange(slice_len, dtype=jnp.int32)
    kernel = matern(my_pts, panel_pts, inv_len)
    kernel = kernel + jnp.where(my_ids[:, None] == panel_ids[None, :], my_nug[:, None], 0.0)
    mine_lower = lax.linalg.triangular_solve(
        factor, kernel, left_side=False, lower=True, transpose_a=True
    )
    row_lower = lax.all_gather(mine_lower, "col", axis=0, tiled=True)
    column_ids = (
        jnp.arange(row_count, dtype=jnp.int32)[:, None] * RB
        + col_index * slice_len
        + jnp.arange(slice_len, dtype=jnp.int32)[None, :]
    ).reshape(-1)
    row_ids = row_index * RB + jnp.arange(RB, dtype=jnp.int32)
    tile_kernel = matern(block_pts, column_pts, inv_len)
    tile_kernel = tile_kernel + jnp.where(
        row_ids[:, None] == column_ids[None, :], nugget[:, None], 0.0
    )
    schur_tile = tile_kernel - jnp.dot(
        row_lower,
        lax.all_gather(mine_lower, "row", axis=0, tiled=True).T,
        precision=lax.Precision.HIGHEST,
        preferred_element_type=jnp.float32,
    )
    return (schur_tile[:, None, :], row_lower)


def solution(mesh):
    in_specs = (P("col", "row", None), P("col", "row"), P("col", "row"), P(), P("row"))
    out_specs = (P("row", "col", None), P("row", None))
    return jax.shard_map(body, mesh=mesh, in_specs=in_specs, out_specs=out_specs, check_vma=False)
```

profile of v0, /device:TPU:1, one launch (start us, length us, event | category | flops | bytes accessed | tf_op | source)
XLA Modules:
  0.0 1268.8 jit_solution(574004869830030400)
XLA Ops:
  9.7 8.8 collective-permute-start
  18.8 4.9 collective-permute-start.4
  25.1 133.5 %psum.23 = f32[1024]{0:T(1024)S(1)} all-reduce(f32[1024]{0:T(1024)S(1)} %multiply_dynamic-update-slice_fusion), channel_id=1, replica_groups=mesh['row'=64,'col'=8] {'row'}, use_global_device_ids=true, to_apply=%region_8.9 | all-reduce | flops 1024 | bytes 8192 | tf_op jit(solution)/shard_map/psum | solution.py:101
  158.9 1.9 collective-permute-start.1
  161.6 1.7 collective-permute-done.1
  163.7 1.9 collective-permute-start.2
  165.6 5.8 collective-permute-start.5
  172.8 2.2 collective-permute-start.6
  175.0 1.9 collective-permute-start.3
  178.1 1.9 collective-permute-start.7
  180.2 2.3 collective-permute-done.7
  182.7 47.6 %psum.21 = f32[128,64]{0,1:T(8,128)S(1)} all-reduce(f32[128,64]{0,1:T(8,128)S(1)} %fusion.57), channel_id=1, replica_groups=mesh['row'=64,'col'=8] {'col'}, use_global_device_ids=true, to_apply=%region_2.3 | all-reduce | flops 8192 | bytes 65536 | tf_op jit(solution)/shard_map/psum | solution.py:89
  232.2 95.3 %all_gather.9 = f32[1024,64]{1,0:T(8,128)S(1)} all-gather(f32[16,64]{1,0:T(8,128)S(1)} %copy.58), channel_id=1, replica_groups=mesh['row'=64,'col'=8] {'row'}, dimensions={0}, use_global_device_ids=true | all-gather | bytes 266240 | tf_op jit(solution)/shard_map/all_gather | solution.py:103
  327.5 449.3 %all-reduce.3.cloned.1.call-done = f32[1024,64]{1,0:T(8,128)} async-done(((f32[1024,64]{1,0:T(8,128)}), f32[1024,64]{1,0:T(8,128)}) %all-reduce.3.cloned.1.call-update) | async-done | bytes 262160 | tf_op jit(solution)/shard_map/psum | solution.py:101
  776.8 1.4 multiply_reduce_fusion.1
  778.2 9.5 broadcast_add_fusion
  787.7 5.3 copy.60
  793.1 5.4 copy.61
  798.4 9.3 add_multiply_fusion
  807.7 1.9 copy-done.1
  809.6 11.7 cholesky.222
  821.4 2.5 cholesky.254
  823.9 9.8 custom-call.62
  833.7 2.4 constant_dynamic-update-slice_fusion.31
  836.1 1.5 convolution_subtract_fusion.1
  837.6 11.7 cholesky.243
  850.0 9.9 custom-call.63
  859.9 1.2 convolution_dynamic-update-slice_fusion
  861.2 2.1 convolution_subtract_fusion.2
  863.3 11.7 cholesky.466
  876.3 9.8 custom-call.64
  887.2 2.3 convolution_subtract_fusion.3
  889.6 11.9 cholesky.485
  902.8 9.8 custom-call.65
  913.7 2.3 convolution_subtract_fusion.4
  916.1 11.7 cholesky.504
  929.1 9.8 custom-call.66
  939.9 2.7 convolution_subtract_fusion.5
  942.6 11.7 cholesky.524
  955.6 9.8 custom-call.67
  966.4 2.0 convolution_subtract_fusion.6
  968.4 11.7 cholesky.544
  981.4 10.0 custom-call.68
  992.2 1.8 convolution_subtract_fusion.7
  994.0 11.7 cholesky.562
  1012.5 4.8 select_select_fusion
  1017.4 23.0 %while.1 = (s32[]{:T(128)}, f32[1024,1024]{1,0:T(8,128)}, s32[8,2]{0,1:T(2,128)S(1)}, f32[8,128,128]{2,1,0:T(8,128)S(1)}, s32[]{:T(128)}) while((s32[]{:T(128)}, f32[1024,1024]{1,0:T(8,128)}, s32[8,2]{0,1:T(2,128)S(1)}, f32[8,128,128]{2,1,0:T(8,128)S(1)}, s32[]{:T(128)}) %tuple.79), condition=%wide.while_cond, body=%wide.while_body.sunk | while | flops 2 | bytes 131189 | solution.py:112
  1018.0 2.3 bitcast_dynamic-update-slice_fusion.2
  1020.9 2.3 bitcast_dynamic-update-slice_fusion.2
  1023.7 2.3 bitcast_dynamic-update-slice_fusion.2
  1026.6 2.3 bitcast_dynamic-update-slice_fusion.2
  1029.5 2.3 bitcast_dynamic-update-slice_fusion.2
  1032.4 2.3 bitcast_dynamic-update-slice_fusion.2
  1035.3 2.3 bitcast_dynamic-update-slice_fusion.2
  1038.1 2.2 bitcast_dynamic-update-slice_fusion.2
  1040.4 78.6 %custom-call.69 = f32[8,128,128]{1,2,0:T(8,128)S(1)} custom-call(f32[8,128,128]{2,1,0:T(8,128)S(1)} %get-tuple-element.9), custom_call_target="InvertDiagBlocksLowerTriangular" | custom-call | tf_op jit(solution)/shard_map/triangular_solve | solution.py:112
  1122.3 1.3 convolution_subtract_fusion.9
  1125.2 1.4 convolution_subtract_fusion.14
  1126.8 1.4 convolution_subtract_fusion.13
  1128.4 1.5 convolution_subtract_fusion.12
  1130.9 39.5 %all_gather.10 = f32[128,1024]{1,0:T(8,128)S(1)} all-gather(f32[16,1024]{1,0:T(8,128)} %copy-done.4), channel_id=1, replica_groups=mesh['row'=64,'col'=8] {'col'}, dimensions={0}, use_global_device_ids=true | all-gather | bytes 589824 | tf_op jit(solution)/shard_map/all_gather | solution.py:115
  1171.3 81.7 %all-gather.2.cloned.1.call-done = f32[1024,1024]{1,0:T(8,128)} async-done(((f32[16,1024]{1,0:T(8,128)}), f32[1024,1024]{1,0:T(8,128)}) %all-gather.2.cloned.1.call-update) | async-done | bytes 4194320 | tf_op jit(solution)/shard_map/all_gather | solution.py:128
  1253.0 6.5 fusion
  1259.6 1.3 copy.62
  (130 shorter events, 36.6 us)
Async XLA Ops:
  7.2 11.4 copy-start
  7.2 769.7 %all-reduce.3.cloned.1.call-start = ((), (), s32[]{:S(2)}) async-start(), calls=%async_computation | async-start | bytes 1048576 | tf_op jit(solution)/shard_map/psum | solution.py:101
  9.7 148.9 %collective-permute-start = (f32[8,1,2]{0,2,1:T(2,128)S(1)}, f32[8,1,2]{0,2,1:T(2,128)S(1)}, u32[]{:S(2)}, u32[]{:S(2)}) collective-permute-start(f32[8,1,2]{0,2,1:T(2,128)S(1)} %bitcast.189), channel_id=1, source_target_pairs={{8,0},{16,8},{24,16},{32,24},{40,32},{48,40},{56,48},{64,56},{72,6... | collective-permute-start | bytes 200 | tf_op jit(solution)/shard_map/ppermute | solution.py:17
  18.8 146.8 %collective-permute-start.4 = (f32[8,1,2,64]{3,0,2,1:T(8,128)S(1)}, f32[8,1,2,64]{3,0,2,1:T(8,128)S(1)}, u32[]{:S(2)}, u32[]{:S(2)}) collective-permute-start(f32[8,1,2,64]{3,0,2,1:T(8,128)S(1)} %get-tuple-element.63), channel_id=1, source_target_pairs={{8,0},{16,8},{24,16},{32,24},{40,32},{48,40},{56,48},{64,56},{72,6... | collective-permute-start | bytes 12296 | tf_op jit(solution)/shard_map/ppermute | solution.py:17
  158.9 4.3 collective-permute-start.1
  163.7 7.8 collective-permute-start.2
  165.6 7.1 collective-permute-start.5
  172.8 5.3 collective-permute-start.6
  175.0 5.0 collective-permute-start.3
  178.1 4.4 collective-permute-start.7
  231.2 0.8 copy-start.3
  232.0 1021.0 %all-gather.2.cloned.1.call-start = ((), (), s32[]{:S(2)}) async-start(), calls=%async_computation.1 | async-start | bytes 4259840 | tf_op jit(solution)/shard_map/all_gather | solution.py:128
  807.7 1.9 copy-start.1
  1012.5 106.5 %copy-start.2 = (f32[1024,64]{1,0:T(8,128)S(1)}, f32[1024,64]{1,0:T(8,128)}, u32[]{:S(2)}) copy-start(f32[1024,64]{1,0:T(8,128)} %all-reduce.3.cloned.1.call-done) | copy-start | bytes 786436
  1017.4 235.7 %copy-start.5 = (f32[128]{0:T(128)S(1)}, f32[128]{0:T(128)}, u32[]{:S(2)}) copy-start(f32[128]{0:T(128)} %param.9) | copy-start | bytes 1540
  1130.1 0.7 copy-start.4
Sparse Core Ops, SparseCore 0:
  232.1 544.6 all-reduce.2
  1130.9 122.0 all-gather.1
where the time goes:
time: 1280 us; the launch traced here: 1270 us
  waiting for transfers between devices  537 us (42%)
  blocking collectives  316 us (25%)
  other arithmetic  270 us (21%)
  matrix products  51.9 us (4%)
  local copies, waits for them, and re-layouts  44.2 us (3%)
  starting transfers between devices  29.4 us (2%)
  between operations  20.3 us (2%)
    psum x1, waiting for transfers between devices, body(): panel_pts, panel_nug = lax.psum((panel_buf, nugget_buf), 'row')  449 us
    another operation x30, other arithmetic, body(): factor = jnp.linalg.cholesky(panel_kernel)  172 us
    psum x1, blocking collectives, body(): panel_pts, panel_nug = lax.psum((panel_buf, nugget_buf), 'row')  133 us
    all_gather x1, blocking collectives, body(): lax.all_gather(my_pts, 'row', axis=0, tiled=True)  95.3 us
    another operation x3, other arithmetic, body(): lax.linalg.triangular_solve(factor, kernel, left_side=False, lower=True,...  83.4 us
    all_gather x1, waiting for transfers between devices, body(): lax.all_gather(mine_lower, 'row', axis=0, tiled=True)  81.7 us
    psum x1, blocking collectives, body(): block_pts = lax.psum(partial_block, 'col')  47.6 us
    all_gather x1, blocking collectives, body(): row_lower = lax.all_gather(mine_lower, 'col', axis=0, tiled=True)  39.5 us
  transfers between devices with their start and end apart: 10, of which 6 were waited for; matrix products, arithmetic and copies ran while one was open for 0% of the time, Pallas kernels for 0%

commit v1 on v0

v1 whole, which is shorter than its diff:
```python
import functools

import jax
import jax.numpy as jnp
from jax import lax
from jax.experimental import pallas as pl
from jax.experimental.pallas import tpu as pltpu
from jax.sharding import PartitionSpec as P

F = 64
PB = 1024
RB = 128
NR = 64
NC = 8
SL = 16
WIN = 16
SLOTS = 32
HI = lax.Precision.HIGHEST
MESH = pl.DeviceIdType.MESH

root_three = 1.7320508075688772


def hdot(a, b):
    return jnp.dot(a, b, precision=HI, preferred_element_type=jnp.float32)


def exchange_kernel(
    tel_ref, tgt_ref, cnt_ref, nug_ref,
    blk_ref, col_ref, pan_ref, pnug_ref,
    out1, in1, comp, gath, mine, nugtile,
    s1, r1, s2, r2, s3, r3, s4, r4, s5, r5,
):
    r = lax.axis_index("row")
    c = lax.axis_index("col")

    def at_row(peer):
        return (peer, c)

    def at_col(peer):
        return (r, peer)

    barrier = pltpu.get_barrier_semaphore()

    def greet_row(i, carry):
        pl.semaphore_signal(
            barrier, inc=1, device_id=at_row(lax.rem(r + i, NR)), device_id_type=MESH
        )
        return carry

    def greet_col(i, carry):
        pl.semaphore_signal(
            barrier, inc=1, device_id=at_col(lax.rem(c + i, NC)), device_id_type=MESH
        )
        return carry

    lax.fori_loop(1, NR, greet_row, 0)
    lax.fori_loop(1, NC, greet_col, 0)

    tel = tel_ref[0]
    t_row = tgt_ref[...]
    sub = lax.broadcasted_iota(jnp.int32, (SLOTS, SLOTS), 0)
    lane = lax.broadcasted_iota(jnp.int32, (SLOTS, SLOTS), 1)
    t_mat = jnp.broadcast_to(t_row, (SLOTS, SLOTS))
    t_col = jnp.sum(jnp.where(sub == lane, t_mat, 0), axis=1, keepdims=True)
    zone_row = lax.shift_right_logical(t_row, 7)
    zone_col = lax.shift_right_logical(t_col, 7)
    filled = cnt_ref[...]
    earlier = (zone_col == zone_row) & (sub < filled) & (sub < lane)
    position = jnp.sum(earlier.astype(jnp.int32), axis=0, keepdims=True)
    offset = jnp.bitwise_and(r - zone_row + NR, NR - 1)
    used = (lane[0:1] < filled) & (position < 2) & (offset < WIN)
    slot = jnp.where(used, offset * 2 + position, -1)
    place = jnp.bitwise_and(t_row, RB - 1).astype(jnp.float32)
    dist = lax.broadcasted_iota(jnp.int32, (WIN, SLOTS), 0) * 2
    pick0 = dist == slot
    pick1 = dist + 1 == slot
    feat0 = hdot(pick0.astype(jnp.float32), tel)
    feat1 = hdot(pick1.astype(jnp.float32), tel)
    place0 = jnp.max(jnp.where(pick0, place, -1.0), axis=1, keepdims=True)
    place1 = jnp.max(jnp.where(pick1, place, -1.0), axis=1, keepdims=True)
    feats = jnp.concatenate([feat0, feat1], axis=1)
    lane_w = lax.broadcasted_iota(jnp.int32, (WIN, 128), 1)
    places = jnp.where(lane_w < F, place0, place1)
    tile_row = lax.broadcasted_iota(jnp.int32, (8, 128), 0)
    for d in range(WIN):
        out1[d] = jnp.where(
            tile_row == 0, feats[d : d + 1], jnp.where(tile_row == 1, places[d : d + 1], 0.0)
        )
    in1[0] = out1[0]
    nugtile[...] = jnp.broadcast_to(nug_ref[...], (8, 128))

    pl.semaphore_wait(barrier, NR - 1 + NC - 1)

    def step1(d):
        return pltpu.make_async_remote_copy(
            src_ref=out1.at[d], dst_ref=in1.at[d], send_sem=s1.at[d], recv_sem=r1.at[d],
            device_id=at_row(lax.rem(r - d + NR, NR)), device_id_type=MESH,
        )

    def start1(d, carry):
        step1(d).start()
        return carry

    lax.fori_loop(1, WIN, start1, 0)

    def step5(i, slot_id):
        return pltpu.make_async_remote_copy(
            src_ref=nugtile, dst_ref=pnug_ref.at[slot_id], send_sem=s5.at[i],
            recv_sem=r5.at[slot_id],
            device_id=at_row(lax.rem(r + i, NR)), device_id_type=MESH,
        )

    @pl.when(r < NC)
    def _():
        def start5(i, carry):
            step5(i, r).start()
            return carry

        lax.fori_loop(1, NR, start5, 0)
        pnug_ref[r] = nugtile[...]

    def wait1(d, carry):
        step1(d).wait_recv()
        return carry

    lax.fori_loop(1, WIN, wait1, 0)
    o = lax.broadcasted_iota(jnp.int32, (2 * WIN, 128), 0)
    k = lax.broadcasted_iota(jnp.int32, (2 * WIN, 128), 1)
    chosen = k == jnp.where(o < WIN, 8 * o, 8 * (o - WIN) + 1)
    comp[...] = hdot(chosen.astype(jnp.float32), in1[...].reshape(WIN * 8, 128))
    gath[c] = comp[...]

    def step2(i, slot_id):
        return pltpu.make_async_remote_copy(
            src_ref=comp, dst_ref=gath.at[slot_id], send_sem=s2.at[i], recv_sem=r2.at[slot_id],
            device_id=at_col(lax.rem(c + i, NC)), device_id_type=MESH,
        )

    for i in range(1, NC):
        step2(i, c).start()
    for i in range(1, NC):
        step2(i, lax.rem(c + i, NC)).wait_recv()

    all_feats = gath[:, 0:WIN, :].reshape(NC * WIN, 128)
    all_places = gath[:, WIN : 2 * WIN, :].reshape(NC * WIN, 128)
    spot = lax.broadcasted_iota(jnp.int32, (NC * WIN, RB), 1).astype(jnp.float32)
    put0 = (all_places[:, 0:1] == spot).astype(jnp.float32)
    put1 = (all_places[:, F : F + 1] == spot).astype(jnp.float32)
    blk_ref[...] = hdot(put0.T, all_feats[:, 0:F]) + hdot(put1.T, all_feats[:, F : 2 * F])

    mine[:, 0:F] = blk_ref[pl.ds(c * SL, 8), :]
    mine[:, F : 2 * F] = blk_ref[pl.ds(c * SL + 8, 8), :]
    col_ref[r] = mine[...]

    def step3(i, slot_id):
        return pltpu.make_async_remote_copy(
            src_ref=mine, dst_ref=col_ref.at[slot_id], send_sem=s3.at[i], recv_sem=r3.at[slot_id],
            device_id=at_row(lax.rem(r + i, NR)), device_id_type=MESH,
        )

    def start3(i, carry):
        step3(i, r).start()
        return carry

    lax.fori_loop(1, NR, start3, 0)

    def wait3(slot_id):
        @pl.when(slot_id != r)
        def _():
            step3(1, slot_id).wait_recv()

    for slot_id in range(NC):
        wait3(slot_id)

    def step4(i, slot_id):
        return pltpu.make_async_remote_copy(
            src_ref=col_ref.at[pl.ds(0, NC)], dst_ref=pan_ref.at[slot_id], send_sem=s4.at[i],
            recv_sem=r4.at[slot_id],
            device_id=at_col(lax.rem(c + i, NC)), device_id_type=MESH,
        )

    for i in range(1, NC):
        step4(i, c).start()
    pan_ref[c] = col_ref[0:NC]

    def rest3(slot_id, carry):
        wait3(slot_id)
        return carry

    lax.fori_loop(NC, NR, rest3, 0)
    for slot_id in range(NC):
        @pl.when(slot_id != r)
        def _(slot_id=slot_id):
            step5(1, slot_id).wait_recv()

    for i in range(1, NC):
        step4(i, lax.rem(c + i, NC)).wait_recv()

    def sent1(d, carry):
        step1(d).wait_send()
        return carry

    lax.fori_loop(1, WIN, sent1, 0)
    for i in range(1, NC):
        step2(i, c).wait_send()
        step4(i, c).wait_send()

    def sent3(i, carry):
        step3(i, r).wait_send()
        return carry

    lax.fori_loop(1, NR, sent3, 0)

    @pl.when(r < NC)
    def _():
        def sent5(i, carry):
            step5(i, r).wait_send()
            return carry

        lax.fori_loop(1, NR, sent5, 0)


def exchange(telemetry, target, counts, nugget):
    dma = pltpu.SemaphoreType.DMA
    vmem = pl.BlockSpec(memory_space=pltpu.VMEM)
    f32 = jnp.float32
    return pl.pallas_call(
        exchange_kernel,
        out_shape=(
            jax.ShapeDtypeStruct((RB, F), f32),
            jax.ShapeDtypeStruct((NR, 8, 128), f32),
            jax.ShapeDtypeStruct((NC, NC, 8, 128), f32),
            jax.ShapeDtypeStruct((NC, 8, 128), f32),
        ),
        in_specs=[vmem] * 4,
        out_specs=(vmem,) * 4,
        scratch_shapes=[
            pltpu.VMEM((WIN, 8, 128), f32),
            pltpu.VMEM((WIN, 8, 128), f32),
            pltpu.VMEM((2 * WIN, 128), f32),
            pltpu.VMEM((NC, 2 * WIN, 128), f32),
            pltpu.VMEM((8, 128), f32),
            pltpu.VMEM((8, 128), f32),
            dma((WIN,)), dma((WIN,)), dma((NC,)), dma((NC,)), dma((NR,)), dma((NR,)),
            dma((NC,)), dma((NC,)), dma((NR,)), dma((NC,)),
        ],
        compiler_params=pltpu.CompilerParams(
            collective_id=0, has_side_effects=True, vmem_limit_bytes=32 * 1024 * 1024
        ),
        name="exchange",
    )(telemetry, target, counts, nugget.reshape(1, RB))


def matern(left, right, inv_len):
    left_s = left * inv_len
    right_s = right * inv_len
    inner = hdot(left_s, right_s.T)
    squared = (
        jnp.sum(left_s * left_s, axis=1)[:, None]
        + jnp.sum(right_s * right_s, axis=1)[None, :]
        - 2.0 * inner
    )
    distance = jnp.sqrt(jnp.maximum(squared, 0.0))
    return (1.0 + root_three * distance) * jnp.exp(-root_three * distance)


def body(telemetry, target, counts, lengthscale, nugget):
    row_index = lax.axis_index("row")
    col_index = lax.axis_index("col")
    block_pts, col_packed, pan_packed, pnug = exchange(telemetry, target, counts, nugget)
    inv_len = 1.0 / lengthscale
    column_pts = col_packed.reshape(NR, 8, 2, F).transpose(0, 2, 1, 3).reshape(PB, F)
    panel_pts = pan_packed.reshape(NC, NC, 8, 2, F).transpose(1, 0, 3, 2, 4).reshape(PB, F)
    panel_nug = pnug[:, 0, :].reshape(PB)
    panel_ids = jnp.arange(PB, dtype=jnp.int32)
    row_ids = row_index * RB + jnp.arange(RB, dtype=jnp.int32)
    column_ids = (
        jnp.arange(NR, dtype=jnp.int32)[:, None] * RB
        + col_index * SL
        + jnp.arange(SL, dtype=jnp.int32)[None, :]
    ).reshape(-1)
    panel_kernel = matern(panel_pts, panel_pts, inv_len) + jnp.diag(panel_nug)
    factor = jnp.linalg.cholesky(panel_kernel)
    kernel = matern(block_pts, panel_pts, inv_len)
    kernel = kernel + jnp.where(row_ids[:, None] == panel_ids[None, :], nugget[:, None], 0.0)
    row_lower = lax.linalg.triangular_solve(
        factor, kernel, left_side=False, lower=True, transpose_a=True
    )
    weights = lax.linalg.triangular_solve(
        factor, row_lower, left_side=False, lower=True, transpose_a=False
    )
    across = matern(column_pts, panel_pts, inv_len)
    across = across + jnp.where(
        column_ids[:, None] == panel_ids[None, :], panel_nug[None, :], 0.0
    )
    tile_kernel = matern(block_pts, column_pts, inv_len)
    tile_kernel = tile_kernel + jnp.where(
        row_ids[:, None] == column_ids[None, :], nugget[:, None], 0.0
    )
    schur_tile = tile_kernel - hdot(weights, across.T)
    return (schur_tile[:, None, :], row_lower)


def solution(mesh):
    in_specs = (P("col", "row", None), P("col", "row"), P("col", "row"), P(), P("row"))
    out_specs = (P("row", "col", None), P("row", None))
    return jax.shard_map(body, mesh=mesh, in_specs=in_specs, out_specs=out_specs, check_vma=False)
```

time: 1280 us -> 435 us (0.34)
  the two profiles are of different devices: /device:TPU:1 before, /device:TPU:71 now
where the time goes in v1:
time: 435 us; the launch traced here: 428 us
  other arithmetic  264 us (61%)
  matrix products  62.8 us (14%)
  local copies, waits for them, and re-layouts  49.8 us (11%)
  Pallas kernels  44.4 us (10%)
  between operations  7.39 us (2%)
    another operation x30, other arithmetic, body(): factor = jnp.linalg.cholesky(panel_kernel)  172 us
    another operation x3, other arithmetic, body(): lax.linalg.triangular_solve(factor, kernel, left_side=False, lower=True,...  83.8 us
    pallas_call x1, Pallas kernels, exchange(): pl.pallas_call(exchange_kernel, out_shape=(jax.ShapeDtypeStruct((RB, F),...  44.4 us
    dot_general x5, matrix products, hdot(): return jnp.dot(a, b, precision=HI, preferred_element_type=jnp.float32)  24.4 us
    another operation x14, matrix products, body(): factor = jnp.linalg.cholesky(panel_kernel)  23.3 us
    another operation x24, local copies, waits for them, and re-layouts  22.8 us
    another operation x15, matrix products, body(): lax.linalg.triangular_solve(factor, kernel, left_side=False, lower=True,...  9.21 us

profile of v1, /device:TPU:71, one launch (start us, length us, event | category | flops | bytes accessed | tf_op | source)
XLA Modules:
  0.0 428.3 jit_solution(17253700126821025766)
XLA Ops:
  2.0 0.7 copy-done
  4.0 44.4 %exchange.1 = (f32[128,64]{1,0:T(8,128)S(1)}, f32[64,8,128]{2,1,0:T(8,128)S(1)}, f32[8,8,8,128]{3,2,1,0:T(8,128)S(1)}, f32[8,8,128]{2,1,0:T(8,128)S(1)}) custom-call(f32[1,32,64]{2,1,0:T(8,128)S(1)} %copy-done, s32[1,32]{1,0:T(1,128)S(1)} %copy-done.1, s32[1,1]{1,0:T(1,128)S(6)} %copy.121.cnt_ref, f32[1,128]{1,0:T(1,128)S(1)} %bitcast.160), custom_call_target="tpu_custom_call" | custom-call | tf_op jit(solution)/shard_map/exchange/pallas_call | solution.py:228
  49.1 9.1 %broadcast_add_fusion = (f32[1024,1024]{0,1:T(8,128)}, f32[1024,1024]{0,1:T(8,128)}, f32[1024,1024]{0,1:T(8,128)}) fusion(f32[1024]{0:T(1024)S(1)} %add.220, f32[1024]{0:T(1024)S(1)} %bitcast.164, f32[1024,64]{1,0:T(8,128)S(1)} %bitcast.161), kind=kOutput, calls=%fused_computation.27 | convolution fusion | flops 816840704 | bytes 12853248 | tf_op jit(solution)/shard_map/dot_general | solution.py:25
  58.2 5.3 %copy.29 = f32[1024,1024]{1,0:T(8,128)} copy(f32[1024,1024]{0,1:T(8,128)} %get-tuple-element.83) | data formatting | bytes 8388608 | tf_op jit(solution)/shard_map/add | solution.py:260
  63.5 5.4 %copy.30 = f32[1024,1024]{1,0:T(8,128)} copy(f32[1024,1024]{0,1:T(8,128)} %get-tuple-element.84) | data formatting | bytes 8388608 | tf_op jit(solution)/shard_map/add | solution.py:283
  68.9 6.3 %add_multiply_fusion = f32[1024,1024]{1,0:T(8,128)S(1)} fusion(f32[1024,1024]{1,0:T(8,128)} %copy.30, f32[1024,1024]{1,0:T(8,128)} %copy.29, f32[1024,1024]{0,1:T(8,128)} %get-tuple-element.87, f32[1024]{0:T(1024)S(1)} %bitcast.165), kind=kLoop, calls=%fused_computation.16 | loop fusion | flops 12582912 | bytes 16781312 | tf_op jit(solution)/shard_map/jit(cholesky)/div | solution.py:284
  75.2 1.9 copy-done.5
  77.1 11.7 %cholesky.222 = f32[128,128]{1,0:T(8,128)S(1)} custom-call(f32[128,128]{1,0:T(8,128)S(1)} %cholesky.577), custom_call_target="Cholesky" | custom-call | tf_op jit(solution)/shard_map/jit(cholesky)/cholesky | solution.py:284
  88.9 9.8 %custom-call.64 = f32[1,128,128]{1,2,0:T(8,128)S(1)} custom-call(f32[1,128,128]{2,1,0:T(8,128)S(1)} %get-tuple-element.82), custom_call_target="InvertDiagBlocksLowerTriangular" | custom-call | tf_op jit(solution)/shard_map/jit(cholesky)/cholesky | solution.py:284
  98.7 2.5 cholesky.254
  101.2 2.4 constant_dynamic-update-slice_fusion.58
  103.6 1.5 convolution_subtract_fusion
  105.1 11.7 %cholesky.243 = f32[128,128]{1,0:T(8,128)S(1)} custom-call(f32[128,128]{1,0:T(8,128)S(1)} %cholesky.581), custom_call_target="Cholesky" | custom-call | tf_op jit(solution)/shard_map/jit(cholesky)/cholesky | solution.py:284
  119.4 10.0 %custom-call.65 = f32[1,128,128]{1,2,0:T(8,128)S(1)} custom-call(f32[1,128,128]{2,1,0:T(8,128)S(1)} %get-tuple-element.79), custom_call_target="InvertDiagBlocksLowerTriangular" | custom-call | tf_op jit(solution)/shard_map/jit(cholesky)/cholesky | solution.py:284
  129.4 1.2 convolution_dynamic-update-slice_fusion
  130.7 2.1 convolution_subtract_fusion.1
  132.8 11.7 %cholesky.466 = f32[128,128]{1,0:T(8,128)S(1)} custom-call(f32[128,128]{1,0:T(8,128)S(1)} %cholesky.586), custom_call_target="Cholesky" | custom-call | tf_op jit(solution)/shard_map/jit(cholesky)/cholesky | solution.py:284
  146.4 9.8 %custom-call.66 = f32[1,128,128]{1,2,0:T(8,128)S(1)} custom-call(f32[1,128,128]{2,1,0:T(8,128)S(1)} %get-tuple-element.76), custom_call_target="InvertDiagBlocksLowerTriangular" | custom-call | tf_op jit(solution)/shard_map/jit(cholesky)/cholesky | solution.py:284
  156.2 1.2 convolution_dynamic-update-slice_fusion.1
  157.4 2.4 convolution_subtract_fusion.2
  159.8 12.1 %cholesky.485 = f32[128,128]{1,0:T(8,128)S(1)} custom-call(f32[128,128]{1,0:T(8,128)S(1)} %cholesky.591), custom_call_target="Cholesky" | custom-call | tf_op jit(solution)/shard_map/jit(cholesky)/cholesky | solution.py:284
  173.8 9.8 %custom-call.67 = f32[1,128,128]{1,2,0:T(8,128)S(1)} custom-call(f32[1,128,128]{2,1,0:T(8,128)S(1)} %get-tuple-element.73), custom_call_target="InvertDiagBlocksLowerTriangular" | custom-call | tf_op jit(solution)/shard_map/jit(cholesky)/cholesky | solution.py:284
  183.7 1.1 convolution_dynamic-update-slice_fusion.2
  184.8 2.3 convolution_subtract_fusion.3
  187.1 11.7 %cholesky.504 = f32[128,128]{1,0:T(8,128)S(1)} custom-call(f32[128,128]{1,0:T(8,128)S(1)} %cholesky.596), custom_call_target="Cholesky" | custom-call | tf_op jit(solution)/shard_map/jit(cholesky)/cholesky | solution.py:284
  200.8 9.8 %custom-call.68 = f32[1,128,128]{1,2,0:T(8,128)S(1)} custom-call(f32[1,128,128]{2,1,0:T(8,128)S(1)} %get-tuple-element.70), custom_call_target="InvertDiagBlocksLowerTriangular" | custom-call | tf_op jit(solution)/shard_map/jit(cholesky)/cholesky | solution.py:284
  210.6 1.0 convolution_dynamic-update-slice_fusion.3
  211.6 2.5 convolution_subtract_fusion.4
  214.1 11.7 %cholesky.524 = f32[128,128]{1,0:T(8,128)S(1)} custom-call(f32[128,128]{1,0:T(8,128)S(1)} %cholesky.601), custom_call_target="Cholesky" | custom-call | tf_op jit(solution)/shard_map/jit(cholesky)/cholesky | solution.py:284
  227.8 9.8 %custom-call.69 = f32[1,128,128]{1,2,0:T(8,128)S(1)} custom-call(f32[1,128,128]{2,1,0:T(8,128)S(1)} %get-tuple-element.67), custom_call_target="InvertDiagBlocksLowerTriangular" | custom-call | tf_op jit(solution)/shard_map/jit(cholesky)/cholesky | solution.py:284
  237.6 0.9 convolution_dynamic-update-slice_fusion.4
  238.5 2.0 convolution_subtract_fusion.5
  240.5 11.7 %cholesky.544 = f32[128,128]{1,0:T(8,128)S(1)} custom-call(f32[128,128]{1,0:T(8,128)S(1)} %cholesky.606), custom_call_target="Cholesky" | custom-call | tf_op jit(solution)/shard_map/jit(cholesky)/cholesky | solution.py:284
  254.2 10.0 %custom-call.70 = f32[1,128,128]{1,2,0:T(8,128)S(1)} custom-call(f32[1,128,128]{2,1,0:T(8,128)S(1)} %get-tuple-element.64), custom_call_target="InvertDiagBlocksLowerTriangular" | custom-call | tf_op jit(solution)/shard_map/jit(cholesky)/cholesky | solution.py:284
  264.2 0.8 convolution_dynamic-update-slice_fusion.6
  265.0 1.8 convolution_subtract_fusion.16
  266.8 11.7 %cholesky.562 = f32[128,128]{1,0:T(8,128)S(1)} custom-call(f32[128,128]{1,0:T(8,128)S(1)} %convolution_subtract_fusion.16), custom_call_target="Cholesky" | custom-call | tf_op jit(solution)/shard_map/jit(cholesky)/cholesky | solution.py:284
  280.4 4.8 %select_select_fusion = f32[1024,1024]{1,0:T(8,128)} fusion(f32[1024,1024]{1,0:T(8,128)} %get-tuple-element.62, pred[]{:T(512)S(6)} %cholesky.576), kind=kLoop, calls=%fused_computation.2 | loop fusion | flops 4194304 | bytes 8388609 | tf_op jit(solution)/shard_map/triangular_solve | solution.py:287
  285.3 23.0 %while.1 = (s32[]{:T(128)}, f32[1024,1024]{1,0:T(8,128)}, s32[8,2]{0,1:T(2,128)S(1)}, f32[8,128,128]{2,1,0:T(8,128)S(1)}, s32[]{:T(128)}) while((s32[]{:T(128)}, f32[1024,1024]{1,0:T(8,128)}, s32[8,2]{0,1:T(2,128)S(1)}, f32[8,128,128]{2,1,0:T(8,128)S(1)}, s32[]{:T(128)}) %tuple.75), condition=%wide.while_cond, body=%wide.while_body.sunk | while | flops 2 | bytes 131181 | solution.py:287
  285.9 2.3 bitcast_dynamic-update-slice_fusion.2
  288.7 2.3 bitcast_dynamic-update-slice_fusion.2
  291.6 2.3 bitcast_dynamic-update-slice_fusion.2
  294.5 2.3 bitcast_dynamic-update-slice_fusion.2
  297.4 2.3 bitcast_dynamic-update-slice_fusion.2
  300.3 2.3 bitcast_dynamic-update-slice_fusion.2
  303.2 2.3 bitcast_dynamic-update-slice_fusion.2
  306.0 2.2 bitcast_dynamic-update-slice_fusion.2
  308.2 79.0 %custom-call.71 = f32[8,128,128]{1,2,0:T(8,128)S(1)} custom-call(f32[8,128,128]{2,1,0:T(8,128)S(1)} %get-tuple-element.17), custom_call_target="InvertDiagBlocksLowerTriangular" | custom-call | tf_op jit(solution)/shard_map/triangular_solve | solution.py:287
  387.9 0.9 select_add_fusion.1
  389.1 1.2 convolution_subtract_fusion.15
  390.6 1.3 convolution_subtract_fusion.14
  392.2 1.4 convolution_subtract_fusion.20
  395.8 0.8 convolution_subtract_fusion.12
  396.9 0.9 convolution_subtract_fusion.11
  401.1 0.7 convolution_subtract_fusion.8
  402.1 0.8 convolution_subtract_fusion.7
  403.2 0.9 convolution_subtract_fusion.6
  404.4 0.8 copy-done.6
  405.8 0.8 fusion.21
  406.5 6.3 %maximum_sqrt_fusion = f32[1024,1024]{0,1:T(8,128)} fusion(f32[1024,64]{1,0:T(8,128)S(1)} %bitcast.163, f32[1024,64]{1,0:T(8,128)S(1)} %bitcast.162, f32[1024]{0:T(1024)S(1)} %add.207, f32[1024]{0:T(1024)S(1)} %add.220), kind=kOutput, calls=%fused_computation.15 | convolution fusion | flops 809500672 | bytes 4726784 | tf_op jit(solution)/shard_map/dot_general | solution.py:25
  412.8 5.4 %copy.33 = f32[1024,1024]{1,0:T(8,128)} copy(f32[1024,1024]{0,1:T(8,128)} %maximum_sqrt_fusion) | data formatting | bytes 8388608 | tf_op jit(solution)/shard_map/sqrt | solution.py:264
  418.4 7.4 %fusion.25 = f32[128,1,1024]{2,0,1:T(8,128)S(1)} fusion(f32[128,1024]{0,1:T(8,128)S(1)} %copy-done.7, f32[1024,1024]{1,0:T(8,128)} %copy.33, s32[1024]{0:T(1024)S(1)} %add.218, f32[1024]{0:T(1024)S(1)} %bitcast.166, f32[128,1024]{1,0:T(8,128)S(1)} %fusion.21, f32[128]{0:T(128)S(1)} %copy-done.3, s32[128]{0:T(128)S(1)} %iota_add_fusion.1), kind=kOutput, calls=%fused_computation.39 | convolution fusion | flops 1619001344 | bytes 5776384 | tf_op jit(solution)/shard_map/dot_general | solution.py:25
  425.8 1.3 copy.35
  427.1 1.0 copy.36
  (114 shorter events, 25.0 us)
Async XLA Ops:
  1.9 0.7 copy-start
  2.7 0.7 copy-start.1
  3.3 0.7 copy-start.2
  75.2 1.9 copy-start.5
  285.2 102.7 %copy-start.3 = (f32[128]{0:T(128)S(1)}, f32[128]{0:T(128)}, u32[]{:S(2)}) copy-start(f32[128]{0:T(128)} %param.9) | copy-start | bytes 1540
  387.9 6.0 %copy-start.4 = (f32[1024,1024]{1,0:T(8,128)S(1)}, f32[1024,1024]{1,0:T(8,128)}, u32[]{:S(2)}) copy-start(f32[1024,1024]{1,0:T(8,128)} %get-tuple-element.151) | copy-start | bytes 12582916
  404.4 0.8 copy-start.6
  412.8 5.6 %copy-start.7 = (f32[128,1024]{0,1:T(8,128)S(1)}, f32[128,1024]{0,1:T(8,128)}, u32[]{:S(2)}) copy-start(f32[128,1024]{0,1:T(8,128)} %copy-done.6) | copy-start | bytes 1572868

commit v2 on v1

--- a/solution.py
+++ b/solution.py
@@ -252,53 +252,183 @@
     )(telemetry, target, counts, nugget.reshape(1, RB))
 
 
-def matern(left, right, inv_len):
-    left_s = left * inv_len
-    right_s = right * inv_len
-    inner = hdot(left_s, right_s.T)
+def recip(p):
+    x = pl.reciprocal(p, approx=True)
+    return x * (2.0 - p * x)
+
+
+def factor_block(tile):
+    sub = lax.broadcasted_iota(jnp.int32, (8, RB), 0)
+    lane = lax.broadcasted_iota(jnp.int32, (8, RB), 1)
+    for first in range(0, RB, 8):
+        rows = tile[first : first + 8, :]
+        cols = [jnp.broadcast_to(rows[:, first + k : first + k + 1], (8, RB)) for k in range(8)]
+        in_panel = (lane >= first) & (lane < first + 8)
+        rows = jnp.where(in_panel, (lane - first == sub).astype(jnp.float32), rows)
+        pivots = jnp.ones((8, RB), jnp.float32)
+        for i in range(8):
+            top = [jnp.broadcast_to(cols[k][i : i + 1], (8, RB)) for k in range(i, 8)]
+            step = jnp.where(sub > i, cols[i] * recip(top[0]), 0.0)
+            pivots = jnp.where(sub == i, top[0], pivots)
+            for k in range(i + 1, 8):
+                cols[k] = cols[k] - step * top[k - i]
+            if i < 7:
+                rows = rows - step * jnp.broadcast_to(rows[i : i + 1], (8, RB))
+        done = rows * lax.rsqrt(pivots)
+        tile[first : first + 8, :] = done
+        if first + 8 < RB:
+            low = first + 8
+            product = tdot(done, done)
+            lane_l = lax.broadcasted_iota(jnp.int32, (RB - low, RB), 1)
+            rest = jnp.where((lane_l >= first) & (lane_l < low), 0.0, tile[low:, :])
+            tile[low:, :] = rest - product[low:, :]
+
+
+def tdot(a, b):
+    return lax.dot_general(
+        a, b, (((0,), (0,)), ((), ())), precision=HI, preferred_element_type=jnp.float32
+    )
+
+
+def ndot(a, b):
+    return lax.dot_general(
+        a, b, (((1,), (1,)), ((), ())), precision=HI, preferred_element_type=jnp.float32
+    )
+
+
+def matern(left, right):
+    ones = jnp.ones((8, F), jnp.float32)
     squared = (
-        jnp.sum(left_s * left_s, axis=1)[:, None]
-        + jnp.sum(right_s * right_s, axis=1)[None, :]
-        - 2.0 * inner
-    )
-    distance = jnp.sqrt(jnp.maximum(squared, 0.0))
-    return (1.0 + root_three * distance) * jnp.exp(-root_three * distance)
+        jnp.sum(left * left, axis=1, keepdims=True)
+        + ndot(ones, right * right)[0:1]
+        - 2.0 * ndot(left, right)
+    )
+    scaled = root_three * jnp.sqrt(jnp.maximum(squared, 0.0))
+    return (1.0 + scaled) * jnp.exp(-scaled)
+
+
+def factor_kernel(
+    where_ref, blk_ref, col_ref, pan_ref, pnug_ref, nug_ref, len_ref,
+    schur_ref, lower_ref,
+    own, pts, cpts, nugs, big, across, weights, tile,
+):
+    r = where_ref[0]
+    c = where_ref[1]
+    inv = 1.0 / len_ref[...]
+    own[...] = blk_ref[...] * inv
+    for rb in range(NC):
+        nugs[:, rb * RB : (rb + 1) * RB] = pnug_ref[rb]
+        for cc in range(NC):
+            at = rb * RB + cc * SL
+            both = pan_ref[cc, rb]
+            pts[at : at + 8, :] = both[:, 0:F] * inv
+            pts[at + 8 : at + SL, :] = both[:, F : 2 * F] * inv
+    for rb in range(NR):
+        both = col_ref[rb]
+        cpts[rb * SL : rb * SL + 8, :] = both[:, 0:F] * inv
+        cpts[rb * SL + 8 : rb * SL + SL, :] = both[:, F : 2 * F] * inv
+
+    eye = lax.broadcasted_iota(jnp.int32, (RB, RB), 0) == lax.broadcasted_iota(
+        jnp.int32, (RB, RB), 1
+    )
+    sub = lax.broadcasted_iota(jnp.int32, (RB, 1), 0)
+
+    def column_ids():
+        n = lax.broadcasted_iota(jnp.int32, (1, PB), 1)
+        return lax.shift_right_logical(n, 4) * RB + c * SL + jnp.bitwise_and(n, SL - 1)
+
+    for i in range(NC):
+        at = i * RB
+        if i:
+            big[at : at + RB, 0:at] = jnp.zeros((RB, at), jnp.float32)
+        mine = pts[at : at + RB, :]
+        big[at : at + RB, at:PB] = matern(mine, pts[at:, :])
+        nug_here = jnp.where(eye, nugs[0:1, at : at + RB], 0.0)
+        big[at : at + RB, at : at + RB] += nug_here
+        same = jnp.where(r == i, 1.0, 0.0)
+        big[at : at + RB, PB:] = matern(mine, own[...]) + same * nug_here
+
+    def across_rows(i, carry):
+        at = pl.multiple_of(i * RB, RB)
+        nug_col = jnp.sum(
+            jnp.where(eye, nugs[0:1, pl.ds(at, RB)], 0.0), axis=1, keepdims=True
+        )
+        across[pl.ds(at, RB), :] = matern(pts[pl.ds(at, RB), :], cpts[...]) + jnp.where(
+            at + sub == column_ids(), nug_col, 0.0
+        )
+        return carry
+
+    lax.fori_loop(0, NC, across_rows, 0)
+
+    low = lax.broadcasted_iota(jnp.int32, (RB, RB), 0) >= lax.broadcasted_iota(
+        jnp.int32, (RB, RB), 1
+    )
+
+    def eliminate(k, carry):
+        at = pl.multiple_of(k * RB, RB)
+        tile[...] = big[pl.ds(at, RB), pl.ds(at, RB)]
+        factor_block(tile)
+        inverse = jnp.where(low, tile[...], 0.0)
+        big[pl.ds(at, RB), pl.ds(at, RB)] = eye.astype(jnp.float32)
+        upper = hdot(inverse, big[pl.ds(at, RB), :])
+        big[pl.ds(at, RB), :] = upper
+
+        def update(i, carry):
+            to = pl.multiple_of(i * RB, RB)
+            coef = big[pl.ds(at, RB), pl.ds(to, RB)]
+            big[pl.ds(to, RB), pl.ds(at, RB)] = jnp.zeros((RB, RB), jnp.float32)
+            big[pl.ds(to, RB), :] = big[pl.ds(to, RB), :] - tdot(coef, big[pl.ds(at, RB), :])
+            return carry
+
+        lax.fori_loop(k + 1, NC, update, 0)
+        return carry
+
+    lax.fori_loop(0, NC, eliminate, 0)
+
+    for j in range(NC):
+        at = j * RB
+        weights[at : at + RB, :] = tdot(big[at:, at : at + RB], big[at:, PB:])
+        lower_ref[:, at : at + RB] = big[at : at + RB, PB:].T
+    nug_own = jnp.sum(jnp.where(eye, nug_ref[...], 0.0), axis=1, keepdims=True)
+    schur_ref[...] = (
+        matern(own[...], cpts[...])
+        + jnp.where(r * RB + sub == column_ids(), nug_own, 0.0)
+        - tdot(weights[...], across[...])
+    )
+
+
+def factor_and_update(where, blk, col, pan, pnug, nugget, lengthscale):
+    vmem = pl.BlockSpec(memory_space=pltpu.VMEM)
+    f32 = jnp.float32
+    return pl.pallas_call(
+        factor_kernel,
+        out_shape=(
+            jax.ShapeDtypeStruct((RB, PB), f32),
+            jax.ShapeDtypeStruct((RB, PB), f32),
+        ),
+        in_specs=[pl.BlockSpec(memory_space=pltpu.SMEM)] + [vmem] * 6,
+        out_specs=(vmem, vmem),
+        scratch_shapes=[
+            pltpu.VMEM((RB, F), f32),
+            pltpu.VMEM((PB, F), f32),
+            pltpu.VMEM((PB, F), f32),
+            pltpu.VMEM((8, PB), f32),
+            pltpu.VMEM((PB, PB + RB), f32),
+            pltpu.VMEM((PB, PB), f32),
+            pltpu.VMEM((PB, RB), f32),
+            pltpu.VMEM((RB, RB), f32),
+        ],
+        compiler_params=pltpu.CompilerParams(vmem_limit_bytes=48 * 1024 * 1024),
+        name="factor",
+    )(where, blk, col, pan, pnug, nugget.reshape(1, RB), lengthscale.reshape(1, F))
 
 
 def body(telemetry, target, counts, lengthscale, nugget):
-    row_index = lax.axis_index("row")
-    col_index = lax.axis_index("col")
     block_pts, col_packed, pan_packed, pnug = exchange(telemetry, target, counts, nugget)
-    inv_len = 1.0 / lengthscale
-    column_pts = col_packed.reshape(NR, 8, 2, F).transpose(0, 2, 1, 3).reshape(PB, F)
-    panel_pts = pan_packed.reshape(NC, NC, 8, 2, F).transpose(1, 0, 3, 2, 4).reshape(PB, F)
-    panel_nug = pnug[:, 0, :].reshape(PB)
-    panel_ids = jnp.arange(PB, dtype=jnp.int32)
-    row_ids = row_index * RB + jnp.arange(RB, dtype=jnp.int32)
-    column_ids = (
-        jnp.arange(NR, dtype=jnp.int32)[:, None] * RB
-        + col_index * SL
-        + jnp.arange(SL, dtype=jnp.int32)[None, :]
-    ).reshape(-1)
-    panel_kernel = matern(panel_pts, panel_pts, inv_len) + jnp.diag(panel_nug)
-    factor = jnp.linalg.cholesky(panel_kernel)
-    kernel = matern(block_pts, panel_pts, inv_len)
-    kernel = kernel + jnp.where(row_ids[:, None] == panel_ids[None, :], nugget[:, None], 0.0)
-    row_lower = lax.linalg.triangular_solve(
-        factor, kernel, left_side=False, lower=True, transpose_a=True
-    )
-    weights = lax.linalg.triangular_solve(
-        factor, row_lower, left_side=False, lower=True, transpose_a=False
-    )
-    across = matern(column_pts, panel_pts, inv_len)
-    across = across + jnp.where(
-        column_ids[:, None] == panel_ids[None, :], panel_nug[None, :], 0.0
-    )
-    tile_kernel = matern(block_pts, column_pts, inv_len)
-    tile_kernel = tile_kernel + jnp.where(
-        row_ids[:, None] == column_ids[None, :], nugget[:, None], 0.0
-    )
-    schur_tile = tile_kernel - hdot(weights, across.T)
+    where = jnp.stack([lax.axis_index("row"), lax.axis_index("col")]).astype(jnp.int32)
+    schur_tile, row_lower = factor_and_update(
+        where, block_pts, col_packed, pan_packed, pnug, nugget, lengthscale
+    )
     return (schur_tile[:, None, :], row_lower)
 
 

time: 435 us -> 158 us (0.36); the launches traced: 428 us -> 157 us
  other arithmetic: 264 us -> 0.08 us
  Pallas kernels: 44.4 us -> 153 us
  matrix products: 62.8 us -> 0 us
  local copies, waits for them, and re-layouts: 49.8 us -> 2.66 us
  between operations: 7.39 us -> 1.32 us
    another operation x33 -> x1, other arithmetic: 256 us -> 0.08 us  [body(): jnp.stack([lax.axis_index('row'), lax.axis_index('col')]).astype(jnp.int32)]
    pallas_call x0 -> x1, Pallas kernels: none -> 109 us  [factor_and_update(): pl.pallas_call(factor_kernel, out_shape=(jax.ShapeDtypeStruct((RB, PB), f...]
    another operation x44 -> x0, matrix products: 38.4 us -> none  [the longest x14 23.3 us: body(): factor = jnp.linalg.cholesky(panel_kernel)]
    another operation x37 -> x0, local copies, waits for them, and re-layouts: 25.4 us -> none
    dot_general x5 -> x0, matrix products: 24.4 us -> none  [hdot(): return jnp.dot(a, b, precision=HI, preferred_element_type=jnp.float32)]
    add x5 -> x0, local copies, waits for them, and re-layouts: 11 us -> none  [the longest x3 5.6 us: matern(): jnp.sum(left_s * left_s, axis=1)[:, None]]
    div x2 -> x0, other arithmetic: 6.99 us -> none  [the longest x1 6.33 us: body(): factor = jnp.linalg.cholesky(panel_kernel)]
    sqrt x1 -> x0, local copies, waits for them, and re-layouts: 5.4 us -> none  [matern(): distance = jnp.sqrt(jnp.maximum(squared, 0.0))]
where the time goes in v2:
time: 158 us; the launch traced here: 157 us
  Pallas kernels  153 us (97%)
  local copies, waits for them, and re-layouts  2.66 us (2%)
    pallas_call x1, Pallas kernels, factor_and_update(): pl.pallas_call(factor_kernel, out_shape=(jax.ShapeDtypeStruct((RB, PB), f...  109 us
    pallas_call x1, Pallas kernels, exchange(): pl.pallas_call(exchange_kernel, out_shape=(jax.ShapeDtypeStruct((RB, F),...  44.4 us

profile of v2, /device:TPU:71, one launch (start us, length us, event | category | flops | bytes accessed | tf_op | source)
XLA Modules:
  0.0 157.4 jit_solution(13411706956793413827)
XLA Ops:
  0.6 0.0 copy-start
  1.3 0.1 pad_add_fusion.where_ref
  1.4 0.0 copy-start.1
  1.4 0.0 copy-start.2
  1.4 0.0 copy-done
  1.4 0.6 copy-done.1
  2.0 0.0 copy-done.2
  2.0 44.4 %exchange.1 = (f32[128,64]{1,0:T(8,128)S(1)}, f32[64,8,128]{2,1,0:T(8,128)S(1)}, f32[8,8,8,128]{3,2,1,0:T(8,128)S(1)}, f32[8,8,128]{2,1,0:T(8,128)S(1)}) custom-call(f32[1,32,64]{2,1,0:T(8,128)S(1)} %copy-done, s32[1,32]{1,0:T(1,128)S(1)} %copy-done.2, s32[1,1]{1,0:T(1,128)S(6)} %copy.8.cnt_ref, f32[1,128]{1,0:T(1,128)S(1)} %bitcast.6), custom_call_target="tpu_custom_call" | custom-call | tf_op jit(solution)/shard_map/exchange/pallas_call | solution.py:228
  46.4 0.0 copy-start.3
  46.4 0.6 copy-done.3
  47.1 109.0 %factor.1 = (f32[128,1024]{1,0:T(8,128)S(1)}, f32[128,1024]{1,0:T(8,128)}) custom-call(s32[2]{0:T(128)S(1)} %pad_add_fusion.where_ref, f32[128,64]{1,0:T(8,128)S(1)} %get-tuple-element.8.blk_ref, f32[64,8,128]{2,1,0:T(8,128)S(1)} %get-tuple-element.9.col_ref, f32[8,8,8,128]{3,2,1,0:T(8,128)S(1)} %get-tuple-element.10.pan_ref, ...), custom_call_target="tpu_custom_call" | custom-call | tf_op jit(solution)/shard_map/factor/pallas_call | solution.py:403
  156.1 1.3 copy.7
Async XLA Ops:
  0.6 0.8 copy-start
  1.4 0.7 copy-start.1
  1.4 0.7 copy-start.2
  46.4 0.7 copy-start.3
